TPU v7x, 128 devices: a whole 4x4x4 slice. The times are simulated.
128 devices in a mesh: enc: 4 (over x_hi, core), dp: 32 (over x_lo, z, y).
Axes of the slice: x: 4 (x_hi: 2, x_lo: 2; x = x_hi * 2 + x_lo), y: 4, z: 4, core: 2. Of those that a mesh axis runs over, the one named last changes fastest.
Arguments:
- sig_in: bfloat16 [12288, 1152], P('dp'), may hold values from -6 to 6
- sig_gain: float32 [1152], replicated, may hold values from 0.1 to 1.9
- sig_up: bfloat16 [1152, 4304], P(None, 'enc'), may hold values from -0.1875 to 0.1875
- sig_down: bfloat16 [4304, 1152], P('enc'), may hold values from -0.09375 to 0.09375
- cnx_in: bfloat16 [12288, 1536], P('dp'), may hold values from -6 to 6
- cnx_gain: float32 [1536], replicated, may hold values from 0.1 to 1.9
- cnx_up: bfloat16 [1536, 3072], P(None, 'enc'), may hold values from -0.15625 to 0.15625
- cnx_down: bfloat16 [3072, 1536], P('enc'), may hold values from -0.109375 to 0.109375
- pix_in: bfloat16 [12288, 1536], P('dp'), may hold values from -6 to 6
- pix_gain: float32 [1536], replicated, may hold values from 0.1 to 1.9
- pix_up: bfloat16 [1536, 3968], P(None, 'enc'), may hold values from -0.15625 to 0.15625
- pix_down: bfloat16 [3968, 1536], P('enc'), may hold values from -0.09375 to 0.09375
- proj_weight: bfloat16 [4224, 2048], P(None, 'enc'), may hold values from -0.09375 to 0.09375
- owners: int32 [3072, 1], P('dp'), may hold values from 0 to 31; in each aligned block of 96 rows (0 to 95, 96 to 191, ...) at most 6 rows name the same one
- cotangent: bfloat16 [32, 192, 2048], P('dp', None, 'enc'), may hold values from -0.59765625 to 0.59765625
Outputs:
- projected: bfloat16 [32, 192, 2048], P('dp', None, 'enc')
- grad_sig_up: float32 [1152, 4304], P('dp', 'enc')
- grad_sig_down: float32 [4304, 1152], P('enc', 'dp')
- grad_cnx_up: float32 [1536, 3072], P('dp', 'enc')
- grad_cnx_down: float32 [3072, 1536], P('enc', 'dp')
- grad_pix_up: float32 [1536, 3968], P('dp', 'enc')
- grad_pix_down: float32 [3968, 1536], P('enc', 'dp')
- grad_proj: float32 [4224, 2048], P('dp', 'enc')
Inputs may be any that keep to these rules, and one draw needn't show every extreme that they name: `owners`: in each aligned block of 96 rows no owner is named by more than 6 rows, a bound that some block reaches.
All inputs are finite; a program needn't handle non-finite values.
Results may differ from a plain program's by a relative error of at most 0.0065.
Values may be sent and summed in bfloat16 or wider, within the bound.
A program may use at most 192 MiB of HBM per device.

v0:
```python
import functools

import jax
import jax.numpy as jnp
from jax import lax
from jax.experimental import pallas as pl
from jax.experimental.pallas import tpu as pltpu
from jax.sharding import PartitionSpec as P

F32 = jnp.float32
BF16 = jnp.bfloat16
MESH = pl.DeviceIdType.MESH
EPSILON = 1e-06
GRID = 64
ROWS = 384
POOL = 96
CAT = 4224
LLM = 512
CAP = 6
PAD = 16
N_DP = 32
SLOTS = N_DP * PAD
PICK = 48
PROJ_CHUNK = 144
TILE = 256

ENCODERS = ((1152, 1076, 36, "z"), (1536, 768, 48, "y"), (1536, 992, 48, "z"))
OFFSETS = (0, 1152, 2688)
PARTS = (40, 48, 48)
CHUNKS = (80, 96, 96, PROJ_CHUNK)
UNITS = ((0, 0, 512), (0, 512, 640), (1, 0, 768), (2, 0, 512), (2, 512, 512), (3, 0, LLM))
SIG_A, SIG_B, CNX_A, PIX_A, PIX_B, PROJ_A = range(6)
FROM = (0, 2, 3, 1)
FLIPPED = (True, False, True)
SIG, CNX, PIX = 0, 1, 2


def dot(left, right):
    return jnp.dot(left, right, preferred_element_type=F32)


def dot_nt(left, right):
    return lax.dot_general(left, right, (((1,), (1,)), ((), ())), preferred_element_type=F32)


def dot_tn(left, right):
    return lax.dot_general(left, right, (((0,), (0,)), ((), ())), preferred_element_type=F32)


def iota(shape, axis):
    return lax.broadcasted_iota(jnp.int32, shape, axis)


def tiles_of(extent, width):
    return [(start, min(width, extent - start)) for start in range(0, extent, width)]


def kernel(*refs):
    ins = refs[0:3]
    ups_hbm = refs[3:6]
    downs_hbm = refs[6:9]
    proj_hbm, cot_hbm, owners, *gains = refs[9:15]
    projected = refs[15]
    grads = ((refs[16], refs[17]), (refs[18], refs[19]), (refs[20], refs[21]), (refs[22],))
    (
        normed_0, normed_1, normed_2, slope_0, slope_1, slope_2, pact_0, pact_1, pact_2,
        up_0, up_1, up_2, down_0, down_1, down_2, gfeat_0, gfeat_1, gfeat_2,
        land_0, land_1, land_2, land_3, land_4, land_5,
        cross_0, cross_1, cross_2, cross_3, cross_4, cross_5,
        proj, cot, spread, perm, place, out_buf, cot_in, tok_in, tok_grads,
        gpart, gpart_sib, gpart_far, bpart, bpart_sib, bpart_far, concat,
        cols_out, cols_in, choose, picked,
        load_sem, a2a_send, a2a_recv, a2b_send, a2b_recv, gt_send, gt_recv, cols_send, cols_recv,
        colf_send, colf_recv, rows_send, rows_recv, sibs_send, sibs_recv, sum_send, sum_recv,
        gf_send, gf_recv, gfs_send, gfs_recv, rs_send, rs_recv, x_send, x_recv,
    ) = refs[23:]
    normed = (normed_0, normed_1, normed_2)
    slope = (slope_0, slope_1, slope_2)
    pact = (pact_0, pact_1, pact_2)
    up = (up_0, up_1, up_2)
    down = (down_0, down_1, down_2)
    gfeat = (gfeat_0, gfeat_1, gfeat_2)
    land = (land_0, land_1, land_2, land_3, land_4, land_5)
    cross = (cross_0, cross_1, cross_2, cross_3, cross_4, cross_5)

    enc = lax.axis_index("enc")
    dp = lax.axis_index("dp")
    core = lax.rem(enc, 2)
    x = lax.div(dp, 16)
    z = lax.rem(lax.div(dp, 4), 4)
    y = lax.rem(dp, 4)
    sibling = {"enc": enc + 1 - 2 * core, "dp": dp}
    far = {"enc": lax.rem(enc + 2, 4), "dp": dp}
    mirror = {"enc": enc, "dp": (1 - x) * 16 + z * 4 + y}
    position = {"z": z, "y": y}

    def step_to(axis, k):
        if axis == "z":
            return {"enc": enc, "dp": x * 16 + lax.rem(z + k, 4) * 4 + y}
        return {"enc": enc, "dp": x * 16 + z * 4 + lax.rem(y + k, 4)}

    sends = []

    def remote(src, dst, send, recv, device):
        return pltpu.make_async_remote_copy(
            src_ref=src, dst_ref=dst, send_sem=send, recv_sem=recv, device_id=device,
            device_id_type=MESH,
        )

    def send(src, dst, send_sem, recv_sem, device):
        copy = remote(src, dst, send_sem, recv_sem, device)
        copy.start()
        sends.append(copy)
        return copy

    barrier = pltpu.get_barrier_semaphore()

    def greet(k, carry):
        other = {"enc": enc, "dp": lax.rem(dp + k, N_DP)}
        pl.semaphore_signal(barrier, inc=1, device_id=other, device_id_type=MESH)
        return carry

    lax.fori_loop(1, N_DP, greet, 0)
    for other in (sibling, far):
        pl.semaphore_signal(barrier, inc=1, device_id=other, device_id_type=MESH)

    loads = {}

    def load(name, src, dst):
        copy = pltpu.make_async_copy(src, dst, load_sem.at[len(loads)])
        copy.start()
        loads[name] = copy

    load("cot", cot_hbm.at[0], cot)
    for i in (CNX, PIX, SIG):
        load(f"in{i}", ins[i], normed[i].at[0])
    load("proj", proj_hbm, proj)
    for i in (CNX, PIX, SIG):
        load(f"up{i}", ups_hbm[i], up[i])
    for i in (CNX, PIX, SIG):
        load(f"down{i}", downs_hbm[i], down[i])

    for q in range(4):
        pooled = iota((POOL, ROWS), 0)
        origin = lax.shift_right_logical(pooled, 5) * 128 + (q // 2) * 64
        origin = origin + lax.bitwise_and(pooled, 31) * 2 + q % 2
        perm[q * POOL:(q + 1) * POOL, :] = (iota((POOL, ROWS), 1) == origin).astype(BF16)

    wide = iota((N_DP * CAP, SLOTS), 1)
    for h in range(2):
        rank = lax.bitwise_and(wide, PAD - 1) - 8 * h
        target = lax.shift_right_logical(wide, 4) * CAP + rank
        hit = (iota((N_DP * CAP, SLOTS), 0) == target) & (rank >= 0) & (rank < CAP)
        spread[h] = hit.astype(BF16)

    diagonal = iota((POOL, POOL), 0) == iota((POOL, POOL), 1)
    owner_ids = jnp.sum(jnp.where(diagonal, owners[...], 0), axis=1, keepdims=True)
    onehot = (owner_ids == iota((POOL, 128), 1)).astype(F32)
    earlier = (iota((POOL, POOL), 1) < iota((POOL, POOL), 0)).astype(BF16)
    before = dot(earlier, onehot.astype(BF16))
    slot_rank = jnp.sum(onehot * before, axis=1, keepdims=True)
    slot = owner_ids.astype(F32) * float(PAD) + slot_rank
    for h in range(2):
        place[h] = (iota((POOL, SLOTS), 1).astype(F32) == slot + 8.0 * h).astype(BF16)

    loads["cot"].wait()
    left = dot_tn(spread[0], cot[:, 0:256]) + dot_tn(spread[1], cot[:, 256:512])
    out_buf[...] = left.astype(BF16)

    def normalize(i):
        width = ENCODERS[i][0]
        own = normed[i].at[0]
        loads[f"in{i}"].wait()
        for start, size in tiles_of(width, 384):
            block = own[:, start:start + size]
            own[:, start:start + size] = dot(perm[...], block).astype(BF16)
        gain = gains[i][...].reshape(1, width)

        def part(k, carry):
            rows = pl.ds(pl.multiple_of(k * 32, 32), 32)
            total = jnp.zeros((32, width), F32)
            for q in range(4):
                cells = pl.ds(pl.multiple_of(q * POOL + k * 32, 32), 32)
                values = own[cells, :].astype(F32)
                total = total + values
                mean = jnp.mean(values, axis=1, keepdims=True)
                centered = values - mean
                var = jnp.mean(centered * centered, axis=1, keepdims=True)
                own[cells, :] = (centered * lax.rsqrt(var + EPSILON) * gain).astype(BF16)
            bpart[rows, OFFSETS[i]:OFFSETS[i] + width] = (total * 0.0625).astype(BF16)
            return carry

        lax.fori_loop(0, POOL // 32, part, 0)

    half = pl.ds(pl.multiple_of(core * 192, 192), 192)
    plane_a = pl.ds(pl.multiple_of(core * 192, 96), POOL)
    plane_b = pl.ds(pl.multiple_of(core * 192 + POOL, 96), POOL)

    def rows_copy(i, k):
        axis = ENCODERS[i][3]
        src = (0, 0, 2, 1)[k]
        dst = (2, 1, 3, 3)[k]
        part = (half, half, plane_a, plane_b)[k]
        device = step_to(axis, 1 if k % 2 == 0 else 3)
        return remote(normed[i].at[src, part], normed[i].at[dst, part],
                      rows_send.at[i, k], rows_recv.at[i, k], device)

    def start(copy):
        copy.start()
        sends.append(copy)

    def sibling_rows(i, k):
        block = normed[i].at[(2, 1, 3)[k], half]
        start(remote(block, block, sibs_send.at[i, k], sibs_recv.at[i, k], sibling))

    def rows_start(i):
        for k in range(2):
            start(rows_copy(i, k))

    def rows_relay(i):
        for k in range(2):
            rows_copy(i, k).wait_recv()
            start(rows_copy(i, 2 + k))
            sibling_rows(i, k)

    def rows_last(i):
        for k in range(2, 4):
            rows_copy(i, k).wait_recv()
        sibling_rows(i, 2)

    other_half = pl.ds(pl.multiple_of((1 - core) * 192, 192), 192)

    def rows_wait(i, k):
        block = normed[i].at[(2, 1, 3)[k], other_half]
        remote(block, block, sibs_send.at[i, k], sibs_recv.at[i, k], sibling).wait_recv()

    def over_tiles(first, last, body):
        whole = last // TILE

        def one(t, carry):
            body(pl.ds(pl.multiple_of(t * TILE, TILE), TILE), TILE)
            return carry

        lax.fori_loop(first // TILE, whole, one, 0)
        if last > whole * TILE:
            body(slice(whole * TILE, last), last - whole * TILE)

    def forward(i, first, count):
        width, hidden, _, _ = ENCODERS[i]

        def tile(cols, size):
            rows = normed[i][first:first + count].reshape(count * ROWS, width)
            if FLIPPED[i]:
                pre = dot_nt(rows, up[i][cols, :])
            else:
                pre = dot(rows, up[i][:, cols])
            cubic = 0.035677408136300125 * (pre * pre)
            linear = cubic + 0.7978845608028654
            tanh = jnp.tanh(pre * linear)
            upper = 0.5 + 0.5 * tanh
            act = pre * upper
            grad = upper + act * (1.0 - tanh) * (linear + (cubic + cubic))
            slope[i][first:first + count, :, cols] = grad.astype(BF16).reshape(count, ROWS, size)
            for s in range(count):
                cell = [act[s * ROWS + q * POOL:s * ROWS + (q + 1) * POOL] for q in range(4)]
                total = (cell[0] + cell[1]) + (cell[2] + cell[3])
                pact[i][(first + s) * POOL:(first + s + 1) * POOL, cols] = total.astype(BF16)

        for start_at, size in tiles_of(hidden, TILE):
            tile(slice(start_at, start_at + size), size)

    def branch(i):
        width = ENCODERS[i][0]
        for start, size in tiles_of(width, 384):
            cols = slice(OFFSETS[i] + start, OFFSETS[i] + start + size)
            value = dot(pact[i][0:POOL, :], down[i][:, start:start + size]) * 0.25
            bpart[:, cols] = (bpart[:, cols].astype(F32) + value).astype(BF16)

    mine = pl.ds(pl.multiple_of(core * 48, 48), 48)
    theirs = pl.ds(pl.multiple_of(48 - core * 48, 48), 48)

    def sum_start(n, part, near):
        send(part.at[theirs], near, sum_send.at[n, 0], sum_recv.at[n, 0], sibling)

    def sum_cross(n, part, near, distant):
        remote(part.at[theirs], near, sum_send.at[n, 0], sum_recv.at[n, 0], sibling).wait_recv()
        part[mine, :] = (part[mine, :].astype(F32) + near[...].astype(F32)).astype(BF16)
        send(part.at[mine], distant, sum_send.at[n, 1], sum_recv.at[n, 1], far)

    def sum_wait(n, part, distant):
        remote(part.at[mine], distant, sum_send.at[n, 1], sum_recv.at[n, 1], far).wait_recv()

    def gfeat_finish(which):
        for i in which:
            width = ENCODERS[i][0]
            cols = slice(OFFSETS[i], OFFSETS[i] + width)
            total = gpart[mine, cols].astype(F32) + gpart_far[:, cols].astype(F32)
            gfeat[i][mine, :] = total.astype(BF16)
            for k in (1, 3, 2):
                start(gfeat_copy(i, k))
            start(gfeat_sibling(i, 0))

    def gfeat_copy(i, k):
        src = gfeat[i].at[mine]
        rows = pl.ds(pl.multiple_of(FROM[k] * POOL + core * 48, 48), 48)
        return remote(src, gfeat[i].at[rows], gf_send.at[i, k], gf_recv.at[i, k],
                      step_to(ENCODERS[i][3], k))

    def gfeat_sibling(i, k, arriving=False):
        at = (48 - core * 48) if arriving else core * 48
        block = gfeat[i].at[pl.ds(pl.multiple_of(FROM[k] * POOL + at, 48), 48)]
        return remote(block, block, gfs_send.at[i, k], gfs_recv.at[i, k], sibling)

    def gfeat_relay(i):
        for k in (1, 3, 2):
            gfeat_copy(i, k).wait_recv()
            start(gfeat_sibling(i, k))

    def gfeat_wait(i):
        for k in range(4):
            gfeat_sibling(i, k, True).wait_recv()

    def concat_finish():
        sum_wait(1, bpart, bpart_far)
        total = bpart[mine, :].astype(F32) + bpart_far[...].astype(F32)
        concat[mine, :] = total.astype(BF16)
        block = concat.at[mine]
        send(block, block, sum_send.at[1, 2], sum_recv.at[1, 2], sibling)

    def concat_wait():
        block = concat.at[theirs]
        remote(block, block, sum_send.at[1, 2], sum_recv.at[1, 2], sibling).wait_recv()

    def exchange(dst, send_sem, recv_sem):
        def one(k, carry):
            other = lax.rem(dp + k, N_DP)
            src = out_buf.at[pl.ds(pl.multiple_of(other * PAD, PAD), PAD)]
            to = dst.at[pl.ds(pl.multiple_of(dp * PAD, PAD), PAD)]
            device = {"enc": enc, "dp": other}
            remote(src, to, send_sem.at[k], recv_sem.at[k], device).start()
            return carry

        lax.fori_loop(1, N_DP, one, 0)
        here = pl.ds(pl.multiple_of(dp * PAD, PAD), PAD)
        dst[here, :] = out_buf[here, :]

    def exchange_wait(dst, send_sem, recv_sem, arrived):
        def one(k, carry):
            other = lax.rem(dp + k, N_DP) if not arrived else lax.rem(dp + N_DP - k, N_DP)
            src = out_buf.at[pl.ds(pl.multiple_of(other * PAD, PAD), PAD)]
            to = dst.at[pl.ds(pl.multiple_of(other * PAD, PAD), PAD)]
            device = {"enc": enc, "dp": other}
            copy = remote(src, to, send_sem.at[k], recv_sem.at[k], device)
            if arrived:
                copy.wait_recv()
            else:
                copy.wait_send()
            return carry

        lax.fori_loop(1, N_DP, one, 0)

    hold = up + (proj,)
    gpicked = perm
    ring = ("y", "z", "y", "z")

    def choice(rows_out, chunks, first):
        lanes_in = 384 if chunks == 0 else 256
        pieces = []
        for b in range(2 if chunks == 0 else chunks):
            r = iota((PICK, lanes_in), 0)
            at = r + first + b * (192 if chunks == 0 else rows_out)
            pieces.append(((iota((PICK, lanes_in), 1) == at) & (r < rows_out)).astype(BF16))
        return jnp.concatenate(pieces, axis=0)

    def backward(i, after):
        width, hidden, rows_out, axis = ENCODERS[i]
        p = position[axis]
        if axis == "y":
            choose[0:2 * PICK, 0:384] = choice(rows_out, 0, p * rows_out)
            for w in range(4):
                rows = slice(w * 2 * PICK, (w + 1) * 2 * PICK)
                cols = slice(w * 384, (w + 1) * 384)
                window = normed[i][:, :, cols].reshape(4 * ROWS, 384)
                picked[rows, :] = dot_nt(choose[0:2 * PICK, 0:384], window).astype(BF16)
                gpicked[rows, :] = dot_nt(choose[0:2 * PICK, 0:384], gfeat[i][:, cols]).astype(BF16)
        else:
            for xx in range(2):
                first = xx * 16 * rows_out + p * 4 * rows_out
                tile = lax.div(first, 128)
                choose[:, 0:256] = choice(rows_out, 4, first - tile * 128)
                rows = slice(xx * 4 * PICK, (xx + 1) * 4 * PICK)
                cols = pl.ds(pl.multiple_of(tile * 128, 128), 256)
                window = normed[i][:, :, cols].reshape(4 * ROWS, 256)
                picked[rows, :] = dot_nt(choose[:, 0:256], window).astype(BF16)
                gpicked[rows, :] = dot_nt(choose[:, 0:256], gfeat[i][:, cols]).astype(BF16)
        def tile(cols, size):
            grad_act = dot_nt(gfeat[i][...], down[i][cols, :])
            for s in range(4):
                grad = grad_act[s * POOL:(s + 1) * POOL].astype(BF16)
                for q in range(4):
                    cells = slice(q * POOL, (q + 1) * POOL)
                    slope[i][s, cells, cols] = slope[i][s, cells, cols] * grad
            upper = dot(picked[...], slope[i][:, :, cols].reshape(4 * ROWS, size))
            lower = dot(gpicked[...], pact[i][:, cols])
            part = PARTS[i]
            for k in range(8):
                at = (k % 2) * 4 * PICK + (k // 2) * PICK
                rows = slice(at, at + part)
                both = jnp.concatenate([upper[rows], lower[rows]], axis=0).astype(BF16)
                hold[i][2 * k * part:2 * (k + 1) * part, cols] = both

        done = 0
        for last in sorted(after):
            over_tiles(done, last, tile)
            done = last
            for action in after[last]:
                action()

    def chunk(n, b, xx):
        size = CHUNKS[n]
        return pl.ds(pl.multiple_of((b * 2 + xx) * size, size), size)

    def lanes_of(u):
        return pl.ds(UNITS[u][1], UNITS[u][2])

    def ring_copy(u, k):
        n = UNITS[u][0]
        axis = ring[n]
        p = position[axis]
        nxt, opp, prv = lax.rem(p + 1, 4), lax.rem(p + 2, 4), lax.rem(p + 3, 4)
        where = ((opp, 0), (opp, 1), (nxt, 1), (prv, 0), (nxt, 0), (prv, 1))[k]
        device = step_to(axis, 1 if k in (0, 2, 4) else 3)
        src = hold[n].at[chunk(n, *where), lanes_of(u)]
        return remote(src, land[u].at[k], rs_send.at[u, k], rs_recv.at[u, k], device)

    def reduce_start(u):
        for k in range(4):
            start(ring_copy(u, k))

    def reduce_mid(u):
        n = UNITS[u][0]
        p = position[ring[n]]
        for k, b, xx in ((0, lax.rem(p + 1, 4), 0), (1, lax.rem(p + 3, 4), 1)):
            ring_copy(u, k).wait_recv()
            rows = chunk(n, b, xx)
            total = hold[n][rows, lanes_of(u)].astype(F32) + land[u][k].astype(F32)
            hold[n][rows, lanes_of(u)] = total.astype(BF16)
            start(ring_copy(u, 4 + k))

    def cross_copy(u):
        n = UNITS[u][0]
        src = hold[n].at[chunk(n, position[ring[n]], 1 - x), lanes_of(u)]
        return remote(src, cross[u], x_send.at[u], x_recv.at[u], mirror)

    def ring_total(u, xx):
        n = UNITS[u][0]
        value = hold[n][chunk(n, position[ring[n]], xx), lanes_of(u)].astype(F32)
        return value + land[u][3 - xx].astype(F32) + land[u][4 + xx].astype(F32)

    def reduce_cross(u):
        n = UNITS[u][0]
        for k in range(2, 6):
            ring_copy(u, k).wait_recv()
        total = ring_total(u, 1 - x).astype(BF16)
        hold[n][chunk(n, position[ring[n]], 1 - x), lanes_of(u)] = total
        start(cross_copy(u))

    def reduce_end(u):
        n, first, _ = UNITS[u]
        cross_copy(u).wait_recv()
        total = ring_total(u, x) + cross[u][...].astype(F32)
        for k, out in enumerate(grads[n]):
            rows, width = out.shape
            last = min(first + UNITS[u][2], width)
            at = k * CHUNKS[n] // 2
            out[:, first:last] = total[at:at + rows, 0:last - first]

    def columns(a):
        def one(j, out):
            k = core * 4 + j
            index = lax.rem(k, 2) * 16 + lax.div(k, 2) * 4 + a
            r = iota((PROJ_CHUNK, 256), 0)
            hit = (iota((PROJ_CHUNK, 256), 1) == r + index * 4) & (r < 132)
            window = concat[:, pl.ds(pl.multiple_of(index * 128, 128), 256)]
            return dot_nt(hit.astype(BF16), window).astype(BF16)

        return one

    col_half = pl.ds(pl.multiple_of(core * 576, 576), 576)
    col_other = pl.ds(pl.multiple_of(576 - core * 576, 576), 576)

    def lane(pos):
        return slice(pos * 128, (pos + 1) * 128)

    def columns_start():
        for k in range(1, 4):
            one = columns(lax.rem(y + k, 4))

            def fill(j, carry, k=k, one=one):
                rows = pl.ds(pl.multiple_of(j * PROJ_CHUNK, PROJ_CHUNK), PROJ_CHUNK)
                cols_out[k - 1, rows, :] = one(j, None)
                return carry

            lax.fori_loop(0, 4, fill, 0)
            send(cols_out.at[k - 1], cols_in.at[col_half, lane(FROM[k])], cols_send.at[k],
                 cols_recv.at[k], step_to("y", k))
        one = columns(y)

        def fill_own(j, carry):
            rows = pl.ds(pl.multiple_of((core * 4 + j) * PROJ_CHUNK, PROJ_CHUNK), PROJ_CHUNK)
            cols_in[rows, lane(0)] = one(j, None)
            return carry

        lax.fori_loop(0, 4, fill_own, 0)
        block = cols_in.at[col_half, lane(0)]
        send(block, block, colf_send.at[0], colf_recv.at[0], sibling)

    def columns_relay():
        for k in range(1, 4):
            block = cols_in.at[col_half, lane(FROM[k])]
            remote(cols_out.at[k - 1], block, cols_send.at[k], cols_recv.at[k],
                   step_to("y", k)).wait_recv()
            send(block, block, colf_send.at[k], colf_recv.at[k], sibling)

    def columns_wait():
        for k in range(4):
            block = cols_in.at[col_other, lane(FROM[k])]
            remote(block, block, colf_send.at[k], colf_recv.at[k], sibling).wait_recv()

    def token_rows(pos):
        return tok_grads.at[pl.ds(pos * 128, 128)]

    def tokens_copy(k):
        return remote(token_rows(0), token_rows(FROM[k]), gt_send.at[k], gt_recv.at[k],
                      step_to("y", k))

    normalize(CNX)
    pl.semaphore_wait(barrier, N_DP + 1)
    exchange(cot_in, a2a_send, a2a_recv)
    rows_start(CNX)
    normalize(PIX)
    rows_start(PIX)
    normalize(SIG)

    loads["proj"].wait()
    exchange_wait(cot_in, a2a_send, a2a_recv, True)
    own_grads = jnp.concatenate(
        [dot(place[0], cot_in[...]), dot(place[1], cot_in[...])], axis=1
    ).astype(BF16)
    tok_grads[0:128, :] = jnp.concatenate([own_grads, jnp.zeros((32, LLM), BF16)], axis=0)
    for k in range(1, 4):
        start(tokens_copy(k))
    for start_at, size in tiles_of(CAT, 384):
        cols = slice(start_at, start_at + size)
        gpart[:, cols] = (dot_nt(tok_grads[0:POOL, :], proj[cols, :]) * 0.25).astype(BF16)
    sum_start(0, gpart, gpart_sib)

    loads[f"up{CNX}"].wait()
    forward(CNX, 0, 1)
    sum_cross(0, gpart, gpart_sib, gpart_far)
    loads[f"up{PIX}"].wait()
    forward(PIX, 0, 1)
    loads[f"up{SIG}"].wait()
    forward(SIG, 0, 1)
    for i in (CNX, PIX, SIG):
        loads[f"down{i}"].wait()
        branch(i)
    sum_start(1, bpart, bpart_sib)
    rows_relay(CNX)
    rows_relay(PIX)
    sum_cross(1, bpart, bpart_sib, bpart_far)
    sum_wait(0, gpart, gpart_far)
    gfeat_finish((CNX, PIX))
    concat[POOL:128, :] = jnp.zeros((32, CAT), BF16)

    rows_wait(CNX, 0)
    rows_wait(CNX, 1)
    forward(CNX, 1, 2)
    rows_wait(PIX, 0)
    rows_wait(PIX, 1)
    rows_last(CNX)
    forward(PIX, 1, 2)
    rows_start(SIG)
    rows_wait(CNX, 2)
    forward(CNX, 3, 1)
    concat_finish()
    gfeat_finish((SIG,))
    concat_wait()

    exchange_wait(cot_in, a2a_send, a2a_recv, False)
    tokens = jnp.zeros((POOL, LLM), F32)
    for start_at, size in tiles_of(CAT, 384):
        cols = slice(start_at, start_at + size)
        tokens = tokens + dot(concat[0:POOL, cols], proj[cols, :])
    tokens = tokens.astype(BF16)
    left = dot_tn(place[0], tokens[:, 0:256]) + dot_tn(place[1], tokens[:, 256:512])
    out_buf[...] = left.astype(BF16)
    exchange(tok_in, a2b_send, a2b_recv)
    columns_start()
    gfeat_relay(CNX)
    rows_last(PIX)

    def do(action, *args):
        return functools.partial(action, *args)

    gfeat_wait(CNX)
    backward(CNX, {768: (do(reduce_start, CNX_A),)})
    gfeat_relay(PIX)
    rows_wait(PIX, 2)
    forward(PIX, 3, 1)
    columns_relay()
    gfeat_wait(PIX)
    backward(PIX, {
        512: (do(reduce_start, PIX_A), do(rows_relay, SIG), do(reduce_mid, CNX_A)),
        992: (do(reduce_start, PIX_B),),
    })
    for k in range(1, 4):
        tokens_copy(k).wait_recv()
    columns_wait()
    for k in range(8):
        rows = slice(k * PROJ_CHUNK, (k + 1) * PROJ_CHUNK)
        proj[rows, :] = dot(cols_in[rows, :], tok_grads[...]).astype(BF16)
    reduce_start(PROJ_A)
    reduce_mid(PIX_A)
    gfeat_relay(SIG)
    rows_wait(SIG, 0)
    rows_wait(SIG, 1)
    forward(SIG, 1, 2)
    rows_last(SIG)
    reduce_mid(PIX_B)
    rows_wait(SIG, 2)
    forward(SIG, 3, 1)
    reduce_mid(PROJ_A)
    gfeat_wait(SIG)
    backward(SIG, {
        512: (do(reduce_start, SIG_A), do(reduce_cross, CNX_A)),
        1076: (do(reduce_start, SIG_B),),
    })
    reduce_mid(SIG_A)
    reduce_cross(PIX_A)
    reduce_cross(PROJ_A)
    reduce_cross(PIX_B)
    reduce_mid(SIG_B)
    exchange_wait(tok_in, a2b_send, a2b_recv, True)
    projected[:, 0:256] = dot(spread[0], tok_in[...]).astype(BF16)
    projected[:, 256:512] = dot(spread[1], tok_in[...]).astype(BF16)
    reduce_cross(SIG_A)
    reduce_end(CNX_A)
    reduce_end(PIX_A)
    reduce_end(PROJ_A)
    reduce_cross(SIG_B)
    reduce_end(PIX_B)
    reduce_end(SIG_A)
    reduce_end(SIG_B)

    exchange_wait(tok_in, a2b_send, a2b_recv, False)
    for copy in sends:
        copy.wait_send()


def hand_over(*refs):
    for k in range(8):
        refs[8 + k][...] = refs[k][...]


def local(
    sig_in, sig_gain, sig_up, sig_down, cnx_in, cnx_gain, cnx_up, cnx_down,
    pix_in, pix_gain, pix_up, pix_down, proj_weight, owners, cotangent,
):
    any_spec = pl.BlockSpec(memory_space=pl.ANY)
    vmem_spec = pl.BlockSpec(memory_space=pltpu.VMEM)
    vmem = pltpu.VMEM
    dma = pltpu.SemaphoreType.DMA
    widths = [e[0] for e in ENCODERS]
    hiddens = [e[1] for e in ENCODERS]
    scratch = (
        [vmem((4, ROWS, w), BF16) for w in widths]
        + [vmem((4, ROWS, h), BF16) for h in hiddens]
        + [vmem((4 * POOL, h), BF16) for h in hiddens]
        + [vmem((h, w) if f else (w, h), BF16) for w, h, f in zip(widths, hiddens, FLIPPED)]
        + [vmem((h, w), BF16) for w, h in zip(widths, hiddens)]
        + [vmem((4 * POOL, w), BF16) for w in widths]
        + [vmem((6, CHUNKS[n], w), BF16) for n, _, w in UNITS]
        + [vmem((CHUNKS[n], w), BF16) for n, _, w in UNITS]
        + [
            vmem((CAT, LLM), BF16),
            vmem((N_DP * CAP, LLM), BF16),
            vmem((2, N_DP * CAP, SLOTS), BF16),
            vmem((ROWS, ROWS), BF16),
            vmem((2, POOL, SLOTS), BF16),
            vmem((SLOTS, LLM // 2), BF16),
            vmem((SLOTS, LLM // 2), BF16),
            vmem((SLOTS, LLM // 2), BF16),
            vmem((512, LLM), BF16),
            vmem((POOL, CAT), BF16),
            vmem((POOL // 2, CAT), BF16),
            vmem((POOL // 2, CAT), BF16),
            vmem((POOL, CAT), BF16),
            vmem((POOL // 2, CAT), BF16),
            vmem((POOL // 2, CAT), BF16),
            vmem((128, CAT), BF16),
            vmem((3, 4 * PROJ_CHUNK, 128), BF16),
            vmem((8 * PROJ_CHUNK, LLM), BF16),
            vmem((4 * PICK, 384), BF16),
            vmem((8 * PICK, 4 * ROWS), BF16),
        ]
        + [
            dma((11,)),
            dma((N_DP,)), dma((N_DP,)), dma((N_DP,)), dma((N_DP,)),
            dma((4,)), dma((4,)), dma((4,)), dma((4,)), dma((4,)), dma((4,)),
            dma((3, 4)), dma((3, 4)), dma((3, 3)), dma((3, 3)),
            dma((2, 3)), dma((2, 3)),
            dma((3, 4)), dma((3, 4)), dma((3, 4)), dma((3, 4)),
            dma((6, 6)), dma((6, 6)), dma((6,)), dma((6,)),
        ]
    )
    outs = pl.pallas_call(
        kernel,
        out_shape=[
            jax.ShapeDtypeStruct((N_DP * CAP, LLM), BF16),
            *[jax.ShapeDtypeStruct((e[2], e[1]), F32) for e in ENCODERS for _ in range(2)],
            jax.ShapeDtypeStruct((132, LLM), F32),
        ],
        in_specs=[any_spec] * 11 + [vmem_spec] * 4,
        out_specs=[vmem_spec] * 8,
        scratch_shapes=scratch,
        compiler_params=pltpu.CompilerParams(
            collective_id=0, has_side_effects=True, vmem_limit_bytes=64 * 2**20
        ),
        cost_estimate=pl.CostEstimate(flops=2 * 10**10, bytes_accessed=3 * 10**7, transcendentals=0),
    )(
        sig_in, cnx_in, pix_in, sig_up.T, cnx_up, pix_up.T, sig_down, cnx_down, pix_down,
        proj_weight, cotangent, owners.T,
        sig_gain, cnx_gain, pix_gain,
    )
    outs = pl.pallas_call(
        hand_over,
        out_shape=[jax.ShapeDtypeStruct(o.shape, o.dtype) for o in outs],
        in_specs=[vmem_spec] * 8,
        out_specs=[vmem_spec] * 8,
    )(*outs)
    return (outs[0][None], outs[1], outs[2].T, outs[3], outs[4].T, outs[5], outs[6].T, outs[7])


def solution(mesh):
    placed = (
        P("dp", None), P(), P(None, "enc"), P("enc", None),
        P("dp", None), P(), P(None, "enc"), P("enc", None),
        P("dp", None), P(), P(None, "enc"), P("enc", None),
        P(None, "enc"), P("dp", None), P("dp", None, "enc"),
    )
    return jax.shard_map(
        local,
        mesh=mesh,
        in_specs=placed,
        out_specs=(
            P("dp", None, "enc"), P("dp", "enc"), P("enc", "dp"), P("dp", "enc"),
            P("enc", "dp"), P("dp", "enc"), P("enc", "dp"), P("dp", "enc"),
        ),
        check_vma=False,
    )
```

profile of v0, /device:TPU:0, one launch (start us, length us, event | category | flops | bytes accessed | tf_op | source)
XLA Modules:
  0.0 109.9 jit_solution(10758415836699066909)
XLA Ops:
  0.6 106.7 %shard_map.206 = (bf16[192,512]{1,0:T(8,128)(2,1)}, f32[36,1076]{1,0:T(8,128)}, f32[36,1076]{1,0:T(8,128)}, f32[48,768]{1,0:T(8,128)}, f32[48,768]{1,0:T(8,128)}...) custom-call(bf16[384,1152]{1,0:T(8,128)(2,1)} %refs_0_.1, bf16[384,1536]{1,0:T(8,128)(2,1)} %refs_1_.1, ...), custom_call_target="tpu_custom_call" | custom-call | flops 20000000000 | bytes 30000000 | tf_op jit(solution)/shard_map/pallas_call | solution.py:717
  107.3 2.6 %shard_map.207 = (bf16[192,512]{1,0:T(8,128)(2,1)}, f32[36,1076]{1,0:T(8,128)}, f32[36,1076]{1,0:T(8,128)}, f32[48,768]{1,0:T(8,128)}, f32[48,768]{1,0:T(8,128)}...) custom-call(bf16[192,512]{1,0:T(8,128)(2,1)} %get-tuple-element.24.refs_0_, ...), custom_call_target="tpu_custom_call" | custom-call | tf_op jit(solution)/shard_map/pallas_call | solution.py:736
where the time goes:
time: 110 us
  Pallas kernels  109 us (99%)
    pallas_call x1, Pallas kernels, local(): pl.pallas_call(kernel, out_shape=[jax.ShapeDtypeStruct((N_DP * CAP, LLM),...  107 us
    pallas_call x1, Pallas kernels, local(): pl.pallas_call(hand_over, out_shape=[jax.ShapeDtypeStruct(o.shape, o.dtyp...  2.58 us

commit v1 on v0

--- a/solution.py
+++ b/solution.py
@@ -566,9 +566,9 @@
         loads[f"down{i}"].wait()
         branch(i)
     sum_start(1, bpart, bpart_sib)
+    sum_cross(1, bpart, bpart_sib, bpart_far)
     rows_relay(CNX)
     rows_relay(PIX)
-    sum_cross(1, bpart, bpart_sib, bpart_far)
     sum_wait(0, gpart, gpart_far)
     gfeat_finish((CNX, PIX))
     concat[POOL:128, :] = jnp.zeros((32, CAT), BF16)

time: 110 us -> 110 us (level)
  no operation moved by 1% of the time
where the time goes in v1:
time: 110 us
  Pallas kernels  109 us (99%)
    pallas_call x1, Pallas kernels, local(): pl.pallas_call(kernel, out_shape=[jax.ShapeDtypeStruct((N_DP * CAP, LLM),...  107 us
    pallas_call x1, Pallas kernels, local(): pl.pallas_call(hand_over, out_shape=[jax.ShapeDtypeStruct(o.shape, o.dtyp...  2.58 us

profile of v1, /device:TPU:0, one launch (start us, length us, event | category | flops | bytes accessed | tf_op | source)
XLA Modules:
  0.0 109.9 jit_solution(16798442622496735663)
XLA Ops:
  0.6 106.7 %shard_map.206 = (bf16[192,512]{1,0:T(8,128)(2,1)}, f32[36,1076]{1,0:T(8,128)}, f32[36,1076]{1,0:T(8,128)}, f32[48,768]{1,0:T(8,128)}, f32[48,768]{1,0:T(8,128)}...) custom-call(bf16[384,1152]{1,0:T(8,128)(2,1)} %refs_0_.1, bf16[384,1536]{1,0:T(8,128)(2,1)} %refs_1_.1, ...), custom_call_target="tpu_custom_call" | custom-call | flops 20000000000 | bytes 30000000 | tf_op jit(solution)/shard_map/pallas_call | solution.py:717
  107.3 2.6 %shard_map.207 = (bf16[192,512]{1,0:T(8,128)(2,1)}, f32[36,1076]{1,0:T(8,128)}, f32[36,1076]{1,0:T(8,128)}, f32[48,768]{1,0:T(8,128)}, f32[48,768]{1,0:T(8,128)}...) custom-call(bf16[192,512]{1,0:T(8,128)(2,1)} %get-tuple-element.24.refs_0_, ...), custom_call_target="tpu_custom_call" | custom-call | tf_op jit(solution)/shard_map/pallas_call | solution.py:736
